TPU v7x, 32 devices: a whole 2x2x4 slice. The times are simulated.
32 devices in a mesh: row: 8 (over y, x, core), col: 4 (over z).
Axes of the slice: x: 2, y: 2, z: 4, core: 2. Of those that a mesh axis runs over, the one named last changes fastest.
Arguments:
- field: float32 [1, 256, 256, 512], P(None, 'row', 'col'), may hold values from -6 to 6
- shell: int32 [256, 256, 256], P(('row', 'col')), may hold values from 0 to 255
Outputs:
- power_modes: float32 [1, 256, 256, 256], P(None, ('row', 'col'))
- spectrum: float32 [1, 256], replicated
All inputs are finite; a program needn't handle non-finite values.
Results may differ from a plain program's by a relative error of at most 0.0003.
Values sent between devices are 32-bit elements; how exact they have to be, the bound alone decides.
A program may use at most 64 MiB of HBM per device.

v0:
```python
import math

import jax
import jax.numpy as jnp
from jax import lax
from jax.sharding import PartitionSpec as P

SHELLS = 256


HIGH = lax.Precision.HIGHEST


def tables(length, freqs):
    places = lax.iota(jnp.int32, length)
    phase = places[:, None] * freqs[None, :] % length
    angle = phase.astype(jnp.float32) * (2.0 * math.pi / length)
    factor = 1.0 / math.sqrt(length)
    return (jnp.cos(angle) * factor, -jnp.sin(angle) * factor)


def split_three(values):
    upper = values.astype(jnp.bfloat16)
    upper_back = lax.optimization_barrier(upper).astype(jnp.float32)
    rest = values - upper_back
    middle = rest.astype(jnp.bfloat16)
    middle_back = lax.optimization_barrier(middle).astype(jnp.float32)
    lowest = (rest - middle_back).astype(jnp.bfloat16)
    return jnp.concatenate([upper, middle, lowest], axis=0)


def local(field, shell):
    fields, cx, cy, nz = field.shape
    n_row = lax.axis_size("row")
    n_col = lax.axis_size("col")
    nx = cx * n_row
    ny = cy * n_col
    keep = nz // 2
    planes = keep // (n_row * n_col)
    cos_x, sin_x = tables(nx, lax.iota(jnp.int32, nx))
    cos_y, sin_y = tables(ny, lax.iota(jnp.int32, ny))
    slots = lax.iota(jnp.int32, keep)
    col_block = slots // (n_row * planes)
    row_block = slots // planes % n_row
    inner = slots % planes
    freqs = (row_block * n_col + col_block) * planes + inner
    cos_z, sin_z = tables(nz, freqs)
    real = jnp.einsum("fxyz,zk->fxyk", field, cos_z, precision=HIGH)
    imag = jnp.einsum("fxyz,zk->fxyk", field, sin_z, precision=HIGH)
    cos_four = cos_y.reshape(n_col, cy, ny)
    sin_four = sin_y.reshape(n_col, cy, ny)
    a_re = lax.all_to_all(real, "col", split_axis=3, concat_axis=3, tiled=True)
    a_im = lax.all_to_all(imag, "col", split_axis=3, concat_axis=3, tiled=True)
    count = a_re.shape[1]
    a_re = a_re.reshape(fields, count, cy, n_col, keep // n_col)
    a_im = a_im.reshape(fields, count, cy, n_col, keep // n_col)
    o_re = jnp.einsum("fiasm,sak->fimk", a_re, cos_four, precision=HIGH) - jnp.einsum(
        "fiasm,sak->fimk", a_im, sin_four, precision=HIGH
    )
    o_im = jnp.einsum("fiasm,sak->fimk", a_re, sin_four, precision=HIGH) + jnp.einsum(
        "fiasm,sak->fimk", a_im, cos_four, precision=HIGH
    )
    real = o_re
    imag = o_im
    b_re = lax.all_to_all(real, "row", split_axis=2, concat_axis=1, tiled=True)
    b_im = lax.all_to_all(imag, "row", split_axis=2, concat_axis=1, tiled=True)
    o_re = jnp.einsum("fxpi,xk->fpik", b_re, cos_x, precision=HIGH) - jnp.einsum(
        "fxpi,xk->fpik", b_im, sin_x, precision=HIGH
    )
    o_im = jnp.einsum("fxpi,xk->fpik", b_re, sin_x, precision=HIGH) + jnp.einsum(
        "fxpi,xk->fpik", b_im, cos_x, precision=HIGH
    )
    power = o_re * o_re + o_im * o_im
    total = planes * ny * nx
    width = math.gcd(total, 32768)
    flat = power.reshape(fields, total)
    labels = shell.reshape(total)
    shell_ids = lax.iota(jnp.int32, SHELLS)

    def add_block(index, summed):
        start = index * width
        part = lax.dynamic_slice_in_dim(flat, start, width, 1)
        marks = lax.dynamic_slice_in_dim(labels, start, width, 0)
        onehot = (marks[:, None] == shell_ids[None, :]).astype(jnp.bfloat16)
        pieces = split_three(part)
        return summed + jnp.dot(pieces, onehot, preferred_element_type=jnp.float32)

    stacked = lax.fori_loop(
        0, total // width, add_block, jnp.zeros((3 * fields, SHELLS), jnp.float32)
    )
    sums = jnp.sum(stacked.reshape(3, fields, SHELLS), axis=0)
    sums = lax.psum(sums, ("row", "col"))
    spectrum = sums * (float(SHELLS) / (keep * ny * nx))
    return (power, spectrum)


def solution(mesh):
    in_specs = (P(None, "row", "col", None), P(("row", "col"), None, None))
    out_specs = (P(None, ("row", "col"), None, None), P())
    return jax.shard_map(local, mesh=mesh, in_specs=in_specs, out_specs=out_specs, check_vma=False)
```

profile of v0, /device:TPU:0, one launch (start us, length us, event | category | flops | bytes accessed | tf_op | source)
XLA Modules:
  0.0 475.8 jit_solution(10769868327661140343)
XLA Ops:
  0.6 7.5 %fusion.18 = f32[1,32,64,256]{3,2,1,0:T(8,128)S(1)} fusion(f32[1,32,64,512]{3,2,1,0:T(8,128)} %param.4, s32[256]{0:T(256)S(1)} %fusion.84), kind=kOutput, calls=%fused_computation.26 | convolution fusion | flops 3223191552 | bytes 6292480 | tf_op jit(solution)/shard_map/fxyz,zk->fxyk/dot_general | solution.py:48
  8.2 4.5 copy.30
  12.6 5.5 %reshape.142 = f32[4,1,131072]{2,1,0:T(1,128)} reshape(f32[256,1,32,64]{3,2,1,0:T(8,128)} %bitcast.97) | data formatting | bytes 4194304
  18.1 6.5 %all-to-all-start = ((f32[4,1,131072]{2,1,0:T(1,128)}), f32[4,1,131072]{2,1,0:T(1,128)}, u32[]{:S(2)}, u32[]{:S(2)}) async-start(f32[4,1,131072]{2,1,0:T(1,128)} %reshape.142), calls=%async_computation | async-start | bytes 4194304 | tf_op jit(solution)/shard_map/all_to_all | solution.py:52
  24.7 7.5 %fusion.21 = f32[1,32,64,256]{3,2,1,0:T(8,128)S(1)} fusion(f32[1,32,64,512]{3,2,1,0:T(8,128)} %param.4, s32[256]{0:T(256)S(1)} %fusion.84), kind=kOutput, calls=%fused_computation.27 | convolution fusion | flops 3223322624 | bytes 6292480 | tf_op jit(solution)/shard_map/fxyz,zk->fxyk/dot_general | solution.py:49
  32.2 4.5 copy.32
  36.7 5.5 %reshape.144 = f32[4,1,131072]{2,1,0:T(1,128)} reshape(f32[256,1,32,64]{3,2,1,0:T(8,128)} %bitcast.98) | data formatting | bytes 4194304
  42.1 30.8 %all-to-all-done = f32[4,1,131072]{2,1,0:T(1,128)} async-done(((f32[4,1,131072]{2,1,0:T(1,128)}), f32[4,1,131072]{2,1,0:T(1,128)}, u32[]{:S(2)}, u32[]{:S(2)}) %all-to-all-start) | async-done | bytes 2097184 | tf_op jit(solution)/shard_map/all_to_all | solution.py:52
  73.0 4.9 %all-to-all-start.1 = ((f32[4,1,131072]{2,1,0:T(1,128)}), f32[4,1,131072]{2,1,0:T(1,128)}, u32[]{:S(2)}, u32[]{:S(2)}) async-start(f32[4,1,131072]{2,1,0:T(1,128)} %reshape.144), calls=%async_computation.1 | async-start | bytes 4194304 | tf_op jit(solution)/shard_map/all_to_all | solution.py:53
  78.4 7.7 %reduce.2 = f32[4,131072]{1,0:T(4,128)S(1)} reduce(f32[4,1,131072]{2,1,0:T(1,128)} %all-to-all-done, f32[]{:T(128)} %broadcast.278), dimensions={1}, to_apply=%all_to_all.28.reduce_sub_computation | reduce | bytes 4194308 | tf_op jit(solution)/shard_map/all_to_all | solution.py:52
  86.1 4.0 reshape.143
  90.0 6.5 %copy.31 = f32[1,32,64,256]{2,3,1,0:T(8,128)} copy(f32[1,32,64,256]{2,1,0,3:T(8,128)} %bitcast.99) | data formatting | bytes 4194304 | tf_op jit(solution)/shard_map/all_to_all | solution.py:52
  96.6 28.6 %all-to-all-done.1 = f32[4,1,131072]{2,1,0:T(1,128)} async-done(((f32[4,1,131072]{2,1,0:T(1,128)}), f32[4,1,131072]{2,1,0:T(1,128)}, u32[]{:S(2)}, u32[]{:S(2)}) %all-to-all-start.1) | async-done | bytes 2097184 | tf_op jit(solution)/shard_map/all_to_all | solution.py:53
  125.2 7.9 %reduce.3 = f32[4,131072]{1,0:T(4,128)S(1)} reduce(f32[4,1,131072]{2,1,0:T(1,128)} %all-to-all-done.1, f32[]{:T(128)} %broadcast.278), dimensions={1}, to_apply=%all_to_all.29.reduce_sub_computation | reduce | bytes 4194308 | tf_op jit(solution)/shard_map/all_to_all | solution.py:53
  133.1 4.0 reshape.145
  137.1 4.8 %copy.33 = f32[1,32,64,256]{2,3,1,0:T(8,128)S(1)} copy(f32[1,32,64,256]{2,1,0,3:T(8,128)} %bitcast.100) | data formatting | bytes 4194304 | tf_op jit(solution)/shard_map/all_to_all | solution.py:53
  141.8 4.6 fusion.54
  146.5 4.6 fusion.17
  151.2 2.5 copy.34
  153.7 4.2 all-to-all-start.2
  157.9 7.9 %fusion.50 = f32[32,64,256,1]{2,1,3,0:T(8,128)S(1)} fusion(f32[32,64,4,64]{1,3,2,0:T(8,128)} %bitcast.95, s32[4,64]{1,0:T(4,128)S(1)} %multiply_add_fusion.1), kind=kOutput, calls=%fused_computation.63 | convolution fusion | flops 1611661312 | bytes 4195328 | tf_op jit(solution)/shard_map/fiasm,sak->fimk/dot_general | solution.py:60
  165.8 4.7 fusion.16
  170.4 2.6 copy.38
  173.0 11.5 %all-to-all-done.2 = f32[1,32,64,256]{3,1,0,2:T(8,128)S(1)} async-done(((f32[1,32,64,256]{3,1,0,2:T(8,128)}), f32[1,32,64,256]{3,1,0,2:T(8,128)S(1)}, u32[]{:S(2)}, u32[]{:S(2)}) %all-to-all-start.2) | async-done | bytes 2097184 | tf_op jit(solution)/shard_map/all_to_all | solution.py:65
  184.5 4.5 all-to-all-start.3
  189.0 4.0 copy.48
  193.0 1.2 copy.52
  194.2 1.5 copy.36
  195.7 1.9 copy.37
  197.7 4.1 fusion.43
  201.8 4.1 fusion.48
  205.9 9.8 %all-to-all-done.3 = f32[1,32,64,256]{3,1,0,2:T(8,128)} async-done(((f32[1,32,64,256]{3,1,0,2:T(8,128)}), f32[1,32,64,256]{3,1,0,2:T(8,128)}, u32[]{:S(2)}, u32[]{:S(2)}) %all-to-all-start.3) | async-done | bytes 2097184 | tf_op jit(solution)/shard_map/all_to_all | solution.py:66
  215.6 2.8 copy.51
  218.5 1.5 copy.40
  220.0 2.1 copy.41
  222.1 2.8 fusion.45
  225.0 4.3 multiply_add_fusion
  229.3 3.7 reshape.130
  233.1 205.0 %while.14 = (s32[]{:T(128)}, f32[3,256]{1,0:T(4,128)S(1)}, f32[1,524288]{1,0:T(1,128)S(1)}, s32[524288]{0:T(1024)}, s32[]{:T(128)}, /*index=5*/s32[]{:T(128)}, s32[]{:T(128)}, s32[]{:T(128)}) while((s32[]{:T(128)}, f32[3,256]{1,0:T(4,128)S(1)}, f32[1,524288]{1,0:T(1,128)S(1)}, s32[524288]{0:T(1024)}, s32[]{:T(128)}, ...), condition=%wide.region_1.2_spmd.clone, body=%wide.region_0.1_spmd.clone.sunk | while | flops 59573768 | bytes 1317029 | solution.py:88
  233.6 0.9 dynamic_slice.29
  234.5 11.4 %fusion.153 = f32[3,256]{1,0:T(4,128)S(1)} fusion(s32[32768]{0:T(1024)S(1)} %dynamic_slice.29, bf16[1,32768]{1,0:T(2,128)(2,1)S(1)} %subtract_convert_fusion.2, bf16[1,32768]{1,0:T(2,128)(2,1)S(1)} %fusion.152, bf16[1,32768]{1,0:T(2,128)(2,1)S(1)} %dynamic-slice_convert_fusion.2, f32[3,256]{1,0:T(4,128)S(1)} %get-tuple-element.156, pred[]{:T(512)S(6)} %compare.19), kind=kOutput, calls=%fused_computation.4.clone.1 | convolution fusion | flops 59311616 | bytes 333825 | tf_op jit(solution)/shard_map/while/body/eval_jaxpr/dot_general | solution.py:86
  246.4 0.9 dynamic_slice.29
  247.4 11.4 %fusion.153 = f32[3,256]{1,0:T(4,128)S(1)} fusion(s32[32768]{0:T(1024)S(1)} %dynamic_slice.29, bf16[1,32768]{1,0:T(2,128)(2,1)S(1)} %subtract_convert_fusion.2, bf16[1,32768]{1,0:T(2,128)(2,1)S(1)} %fusion.152, bf16[1,32768]{1,0:T(2,128)(2,1)S(1)} %dynamic-slice_convert_fusion.2, f32[3,256]{1,0:T(4,128)S(1)} %get-tuple-element.156, pred[]{:T(512)S(6)} %compare.19), kind=kOutput, calls=%fused_computation.4.clone.1 | convolution fusion | flops 59311616 | bytes 333825 | tf_op jit(solution)/shard_map/while/body/eval_jaxpr/dot_general | solution.py:86
  259.2 0.9 dynamic_slice.29
  260.2 11.4 %fusion.153 = f32[3,256]{1,0:T(4,128)S(1)} fusion(s32[32768]{0:T(1024)S(1)} %dynamic_slice.29, bf16[1,32768]{1,0:T(2,128)(2,1)S(1)} %subtract_convert_fusion.2, bf16[1,32768]{1,0:T(2,128)(2,1)S(1)} %fusion.152, bf16[1,32768]{1,0:T(2,128)(2,1)S(1)} %dynamic-slice_convert_fusion.2, f32[3,256]{1,0:T(4,128)S(1)} %get-tuple-element.156, pred[]{:T(512)S(6)} %compare.19), kind=kOutput, calls=%fused_computation.4.clone.1 | convolution fusion | flops 59311616 | bytes 333825 | tf_op jit(solution)/shard_map/while/body/eval_jaxpr/dot_general | solution.py:86
  272.1 0.9 dynamic_slice.29
  273.0 11.4 %fusion.153 = f32[3,256]{1,0:T(4,128)S(1)} fusion(s32[32768]{0:T(1024)S(1)} %dynamic_slice.29, bf16[1,32768]{1,0:T(2,128)(2,1)S(1)} %subtract_convert_fusion.2, bf16[1,32768]{1,0:T(2,128)(2,1)S(1)} %fusion.152, bf16[1,32768]{1,0:T(2,128)(2,1)S(1)} %dynamic-slice_convert_fusion.2, f32[3,256]{1,0:T(4,128)S(1)} %get-tuple-element.156, pred[]{:T(512)S(6)} %compare.19), kind=kOutput, calls=%fused_computation.4.clone.1 | convolution fusion | flops 59311616 | bytes 333825 | tf_op jit(solution)/shard_map/while/body/eval_jaxpr/dot_general | solution.py:86
  284.9 0.9 dynamic_slice.29
  285.8 11.4 %fusion.153 = f32[3,256]{1,0:T(4,128)S(1)} fusion(s32[32768]{0:T(1024)S(1)} %dynamic_slice.29, bf16[1,32768]{1,0:T(2,128)(2,1)S(1)} %subtract_convert_fusion.2, bf16[1,32768]{1,0:T(2,128)(2,1)S(1)} %fusion.152, bf16[1,32768]{1,0:T(2,128)(2,1)S(1)} %dynamic-slice_convert_fusion.2, f32[3,256]{1,0:T(4,128)S(1)} %get-tuple-element.156, pred[]{:T(512)S(6)} %compare.19), kind=kOutput, calls=%fused_computation.4.clone.1 | convolution fusion | flops 59311616 | bytes 333825 | tf_op jit(solution)/shard_map/while/body/eval_jaxpr/dot_general | solution.py:86
  297.7 0.9 dynamic_slice.29
  298.6 11.4 %fusion.153 = f32[3,256]{1,0:T(4,128)S(1)} fusion(s32[32768]{0:T(1024)S(1)} %dynamic_slice.29, bf16[1,32768]{1,0:T(2,128)(2,1)S(1)} %subtract_convert_fusion.2, bf16[1,32768]{1,0:T(2,128)(2,1)S(1)} %fusion.152, bf16[1,32768]{1,0:T(2,128)(2,1)S(1)} %dynamic-slice_convert_fusion.2, f32[3,256]{1,0:T(4,128)S(1)} %get-tuple-element.156, pred[]{:T(512)S(6)} %compare.19), kind=kOutput, calls=%fused_computation.4.clone.1 | convolution fusion | flops 59311616 | bytes 333825 | tf_op jit(solution)/shard_map/while/body/eval_jaxpr/dot_general | solution.py:86
  310.5 0.9 dynamic_slice.29
  311.4 11.4 %fusion.153 = f32[3,256]{1,0:T(4,128)S(1)} fusion(s32[32768]{0:T(1024)S(1)} %dynamic_slice.29, bf16[1,32768]{1,0:T(2,128)(2,1)S(1)} %subtract_convert_fusion.2, bf16[1,32768]{1,0:T(2,128)(2,1)S(1)} %fusion.152, bf16[1,32768]{1,0:T(2,128)(2,1)S(1)} %dynamic-slice_convert_fusion.2, f32[3,256]{1,0:T(4,128)S(1)} %get-tuple-element.156, pred[]{:T(512)S(6)} %compare.19), kind=kOutput, calls=%fused_computation.4.clone.1 | convolution fusion | flops 59311616 | bytes 333825 | tf_op jit(solution)/shard_map/while/body/eval_jaxpr/dot_general | solution.py:86
  323.3 0.9 dynamic_slice.29
  324.2 11.4 %fusion.153 = f32[3,256]{1,0:T(4,128)S(1)} fusion(s32[32768]{0:T(1024)S(1)} %dynamic_slice.29, bf16[1,32768]{1,0:T(2,128)(2,1)S(1)} %subtract_convert_fusion.2, bf16[1,32768]{1,0:T(2,128)(2,1)S(1)} %fusion.152, bf16[1,32768]{1,0:T(2,128)(2,1)S(1)} %dynamic-slice_convert_fusion.2, f32[3,256]{1,0:T(4,128)S(1)} %get-tuple-element.156, pred[]{:T(512)S(6)} %compare.19), kind=kOutput, calls=%fused_computation.4.clone.1 | convolution fusion | flops 59311616 | bytes 333825 | tf_op jit(solution)/shard_map/while/body/eval_jaxpr/dot_general | solution.py:86
  337.0 11.4 %fusion.153 = f32[3,256]{1,0:T(4,128)S(1)} fusion(s32[32768]{0:T(1024)S(1)} %dynamic_slice.29, bf16[1,32768]{1,0:T(2,128)(2,1)S(1)} %subtract_convert_fusion.2, bf16[1,32768]{1,0:T(2,128)(2,1)S(1)} %fusion.152, bf16[1,32768]{1,0:T(2,128)(2,1)S(1)} %dynamic-slice_convert_fusion.2, f32[3,256]{1,0:T(4,128)S(1)} %get-tuple-element.156, pred[]{:T(512)S(6)} %compare.19), kind=kOutput, calls=%fused_computation.4.clone.1 | convolution fusion | flops 59311616 | bytes 333825 | tf_op jit(solution)/shard_map/while/body/eval_jaxpr/dot_general | solution.py:86
  349.9 11.4 %fusion.153 = f32[3,256]{1,0:T(4,128)S(1)} fusion(s32[32768]{0:T(1024)S(1)} %dynamic_slice.29, bf16[1,32768]{1,0:T(2,128)(2,1)S(1)} %subtract_convert_fusion.2, bf16[1,32768]{1,0:T(2,128)(2,1)S(1)} %fusion.152, bf16[1,32768]{1,0:T(2,128)(2,1)S(1)} %dynamic-slice_convert_fusion.2, f32[3,256]{1,0:T(4,128)S(1)} %get-tuple-element.156, pred[]{:T(512)S(6)} %compare.19), kind=kOutput, calls=%fused_computation.4.clone.1 | convolution fusion | flops 59311616 | bytes 333825 | tf_op jit(solution)/shard_map/while/body/eval_jaxpr/dot_general | solution.py:86
  362.7 11.4 %fusion.153 = f32[3,256]{1,0:T(4,128)S(1)} fusion(s32[32768]{0:T(1024)S(1)} %dynamic_slice.29, bf16[1,32768]{1,0:T(2,128)(2,1)S(1)} %subtract_convert_fusion.2, bf16[1,32768]{1,0:T(2,128)(2,1)S(1)} %fusion.152, bf16[1,32768]{1,0:T(2,128)(2,1)S(1)} %dynamic-slice_convert_fusion.2, f32[3,256]{1,0:T(4,128)S(1)} %get-tuple-element.156, pred[]{:T(512)S(6)} %compare.19), kind=kOutput, calls=%fused_computation.4.clone.1 | convolution fusion | flops 59311616 | bytes 333825 | tf_op jit(solution)/shard_map/while/body/eval_jaxpr/dot_general | solution.py:86
  375.5 11.4 %fusion.153 = f32[3,256]{1,0:T(4,128)S(1)} fusion(s32[32768]{0:T(1024)S(1)} %dynamic_slice.29, bf16[1,32768]{1,0:T(2,128)(2,1)S(1)} %subtract_convert_fusion.2, bf16[1,32768]{1,0:T(2,128)(2,1)S(1)} %fusion.152, bf16[1,32768]{1,0:T(2,128)(2,1)S(1)} %dynamic-slice_convert_fusion.2, f32[3,256]{1,0:T(4,128)S(1)} %get-tuple-element.156, pred[]{:T(512)S(6)} %compare.19), kind=kOutput, calls=%fused_computation.4.clone.1 | convolution fusion | flops 59311616 | bytes 333825 | tf_op jit(solution)/shard_map/while/body/eval_jaxpr/dot_general | solution.py:86
  388.3 11.4 %fusion.153 = f32[3,256]{1,0:T(4,128)S(1)} fusion(s32[32768]{0:T(1024)S(1)} %dynamic_slice.29, bf16[1,32768]{1,0:T(2,128)(2,1)S(1)} %subtract_convert_fusion.2, bf16[1,32768]{1,0:T(2,128)(2,1)S(1)} %fusion.152, bf16[1,32768]{1,0:T(2,128)(2,1)S(1)} %dynamic-slice_convert_fusion.2, f32[3,256]{1,0:T(4,128)S(1)} %get-tuple-element.156, pred[]{:T(512)S(6)} %compare.19), kind=kOutput, calls=%fused_computation.4.clone.1 | convolution fusion | flops 59311616 | bytes 333825 | tf_op jit(solution)/shard_map/while/body/eval_jaxpr/dot_general | solution.py:86
  401.1 11.4 %fusion.153 = f32[3,256]{1,0:T(4,128)S(1)} fusion(s32[32768]{0:T(1024)S(1)} %dynamic_slice.29, bf16[1,32768]{1,0:T(2,128)(2,1)S(1)} %subtract_convert_fusion.2, bf16[1,32768]{1,0:T(2,128)(2,1)S(1)} %fusion.152, bf16[1,32768]{1,0:T(2,128)(2,1)S(1)} %dynamic-slice_convert_fusion.2, f32[3,256]{1,0:T(4,128)S(1)} %get-tuple-element.156, pred[]{:T(512)S(6)} %compare.19), kind=kOutput, calls=%fused_computation.4.clone.1 | convolution fusion | flops 59311616 | bytes 333825 | tf_op jit(solution)/shard_map/while/body/eval_jaxpr/dot_general | solution.py:86
  413.9 11.4 %fusion.153 = f32[3,256]{1,0:T(4,128)S(1)} fusion(s32[32768]{0:T(1024)S(1)} %dynamic_slice.29, bf16[1,32768]{1,0:T(2,128)(2,1)S(1)} %subtract_convert_fusion.2, bf16[1,32768]{1,0:T(2,128)(2,1)S(1)} %fusion.152, bf16[1,32768]{1,0:T(2,128)(2,1)S(1)} %dynamic-slice_convert_fusion.2, f32[3,256]{1,0:T(4,128)S(1)} %get-tuple-element.156, pred[]{:T(512)S(6)} %compare.19), kind=kOutput, calls=%fused_computation.4.clone.1 | convolution fusion | flops 59311616 | bytes 333825 | tf_op jit(solution)/shard_map/while/body/eval_jaxpr/dot_general | solution.py:86
  426.7 11.4 %fusion.153 = f32[3,256]{1,0:T(4,128)S(1)} fusion(s32[32768]{0:T(1024)S(1)} %dynamic_slice.29, bf16[1,32768]{1,0:T(2,128)(2,1)S(1)} %subtract_convert_fusion.2, bf16[1,32768]{1,0:T(2,128)(2,1)S(1)} %fusion.152, bf16[1,32768]{1,0:T(2,128)(2,1)S(1)} %dynamic-slice_convert_fusion.2, f32[3,256]{1,0:T(4,128)S(1)} %get-tuple-element.156, pred[]{:T(512)S(6)} %compare.19), kind=kOutput, calls=%fused_computation.4.clone.1 | convolution fusion | flops 59311616 | bytes 333825 | tf_op jit(solution)/shard_map/while/body/eval_jaxpr/dot_general | solution.py:86
  438.1 36.9 %psum.7 = f32[1,256]{1,0:T(1,128)S(1)} all-reduce(f32[1,256]{1,0:T(1,128)S(1)} %bitcast.108), channel_id=1, replica_groups=mesh['row'=8,'col'=4] {'row','col'}, use_global_device_ids=true, to_apply=%region_3.4 | all-reduce | flops 256 | bytes 2048 | tf_op jit(solution)/shard_map/psum | solution.py:92
  (72 shorter events, 16.7 us)
Async XLA Ops:
  18.1 54.8 %all-to-all-start = ((f32[4,1,131072]{2,1,0:T(1,128)}), f32[4,1,131072]{2,1,0:T(1,128)}, u32[]{:S(2)}, u32[]{:S(2)}) async-start(f32[4,1,131072]{2,1,0:T(1,128)} %reshape.142), calls=%async_computation | async-start | bytes 4194304 | tf_op jit(solution)/shard_map/all_to_all | solution.py:52
  73.0 52.2 %all-to-all-start.1 = ((f32[4,1,131072]{2,1,0:T(1,128)}), f32[4,1,131072]{2,1,0:T(1,128)}, u32[]{:S(2)}, u32[]{:S(2)}) async-start(f32[4,1,131072]{2,1,0:T(1,128)} %reshape.144), calls=%async_computation.1 | async-start | bytes 4194304 | tf_op jit(solution)/shard_map/all_to_all | solution.py:53
  137.1 4.8 %copy-start.2 = (f32[1,32,64,256]{2,3,1,0:T(8,128)S(1)}, f32[1,32,64,256]{2,3,1,0:T(8,128)}, u32[]{:S(2)}) copy-start(f32[1,32,64,256]{2,3,1,0:T(8,128)} %copy.31) | copy-start | bytes 6291460
  141.8 4.7 copy-start
  153.7 30.8 %all-to-all-start.2 = ((f32[1,32,64,256]{3,1,0,2:T(8,128)}), f32[1,32,64,256]{3,1,0,2:T(8,128)S(1)}, u32[]{:S(2)}, u32[]{:S(2)}) async-start(f32[1,32,64,256]{3,1,0,2:T(8,128)} %copy.34), calls=%async_computation.2 | async-start | bytes 4194304 | tf_op jit(solution)/shard_map/all_to_all | solution.py:65
  157.9 7.9 %copy-start.1 = (f32[1,32,64,256]{2,3,1,0:T(8,128)S(1)}, f32[1,32,64,256]{2,3,1,0:T(8,128)}, u32[]{:S(2)}) copy-start(f32[1,32,64,256]{2,3,1,0:T(8,128)} %copy-done) | copy-start | bytes 6291460
  184.5 31.2 %all-to-all-start.3 = ((f32[1,32,64,256]{3,1,0,2:T(8,128)}), f32[1,32,64,256]{3,1,0,2:T(8,128)}, u32[]{:S(2)}, u32[]{:S(2)}) async-start(f32[1,32,64,256]{3,1,0,2:T(8,128)} %copy.38), calls=%async_computation.3 | async-start | bytes 4194304 | tf_op jit(solution)/shard_map/all_to_all | solution.py:66
  222.1 2.9 copy-start.3
  222.1 2.9 copy-start.4
where the time goes:
time: 483 us; the launch traced here: 476 us
  matrix products  234 us (48%)
  waiting for transfers between devices  80.7 us (17%)
  local copies, waits for them, and re-layouts  79.8 us (17%)
  blocking collectives  36.9 us (8%)
  other arithmetic  23 us (5%)
  starting transfers between devices  20.1 us (4%)
    dot_general x16, matrix products, add_block(): return summed + jnp.dot(pieces, onehot, preferred_element_type=jnp.float32)  182 us
    psum x1, blocking collectives, local(): sums = lax.psum(sums, ('row', 'col'))  36.9 us
    all_to_all x1, waiting for transfers between devices, local(): a_re = lax.all_to_all(real, 'col', split_axis=3, concat_axis=3, tiled=True)  30.8 us
    all_to_all x1, waiting for transfers between devices, local(): a_im = lax.all_to_all(imag, 'col', split_axis=3, concat_axis=3, tiled=True)  28.6 us
    unnamed x15, local copies, waits for them, and re-layouts  22.9 us
    dynamic_slice x16, local copies, waits for them, and re-layouts, add_block(): marks = lax.dynamic_slice_in_dim(labels, start, width, 0)  14.7 us
    all_to_all x1, waiting for transfers between devices, local(): b_re = lax.all_to_all(real, 'row', split_axis=2, concat_axis=1, tiled=True)  11.5 us
    all_to_all x1, waiting for transfers between devices, local(): b_im = lax.all_to_all(imag, 'row', split_axis=2, concat_axis=1, tiled=True)  9.78 us
  transfers between devices with their start and end apart: 4, of which 4 were waited for; matrix products, arithmetic and copies ran while one was open for 14% of the time, Pallas kernels for 0%

commit v1 on v0

--- a/solution.py
+++ b/solution.py
@@ -1,8 +1,13 @@
 import math
+
+import functools
 
 import jax
 import jax.numpy as jnp
+import numpy as np
 from jax import lax
+from jax.experimental import pallas as pl
+from jax.experimental.pallas import tpu as pltpu
 from jax.sharding import PartitionSpec as P
 
 SHELLS = 256
@@ -29,7 +34,7 @@
     return jnp.concatenate([upper, middle, lowest], axis=0)
 
 
-def local(field, shell):
+def general(field, shell):
     fields, cx, cy, nz = field.shape
     n_row = lax.axis_size("row")
     n_col = lax.axis_size("col")
@@ -94,6 +99,340 @@
     return (power, spectrum)
 
 
+F32 = jnp.float32
+BF16 = jnp.bfloat16
+MIB = 1 << 20
+STEP = 8
+HALF = 16
+
+
+def waves(length, freqs):
+    phase = np.arange(length)[:, None] * np.asarray(freqs)[None, :] % length
+    angle = phase * (2.0 * np.pi / length)
+    factor = 1.0 / math.sqrt(length)
+    return np.cos(angle) * factor, np.sin(angle) * factor
+
+
+def two_parts(table):
+    upper = table.astype(np.float32).astype(jnp.bfloat16)
+    lower = (table - upper.astype(np.float64)).astype(np.float32).astype(jnp.bfloat16)
+    return upper, lower
+
+
+def halves(values):
+    upper = values.astype(BF16)
+    return upper, (values - upper.astype(F32)).astype(BF16)
+
+
+def dot(a, b):
+    return jnp.dot(a, b, preferred_element_type=F32)
+
+
+def product(a, b):
+    return dot(a[0], b[0]) + (dot(a[1], b[0]) + dot(a[0], b[1]))
+
+
+def greet(n_row, n_col, my_row, my_col):
+    barrier = pltpu.get_barrier_semaphore()
+    for k in range(1, n_col):
+        pl.semaphore_signal(
+            barrier, inc=1, device_id={"col": lax.rem(my_col + k, n_col)}, device_id_type=pl.DeviceIdType.MESH
+        )
+    for k in range(1, n_row):
+        pl.semaphore_signal(
+            barrier, inc=1, device_id={"row": lax.rem(my_row + k, n_row)}, device_id_type=pl.DeviceIdType.MESH
+        )
+    pl.semaphore_wait(barrier, n_col + n_row - 2)
+
+
+def exchange_kernel(n_row, n_col, planes, f_ref, tzh, tzl, tyh, tyl, out_ref, snd1, rcv1, snd2, s1, r1, s2, r2, own):
+    my_row = lax.axis_index("row")
+    my_col = lax.axis_index("col")
+    cx, cy, nz = f_ref.shape
+    ny = cy * n_col
+    width = rcv1.shape[3]
+    half = width // 2
+    steps = cx // STEP
+
+    def col_copy(q, k):
+        xs = pl.ds(pl.multiple_of(q * STEP, STEP), STEP)
+        dest = lax.rem(my_col + k, n_col)
+        return pltpu.make_async_remote_copy(
+            src_ref=snd1.at[dest, xs],
+            dst_ref=rcv1.at[my_col, xs],
+            send_sem=s1.at[q, k],
+            recv_sem=r1.at[q, k],
+            device_id={"col": dest},
+            device_id_type=pl.DeviceIdType.MESH,
+        )
+
+    def row_copy(q, k):
+        dest = lax.rem(my_row + k, n_row)
+        there = pl.ds(pl.multiple_of(my_row * cx + q * STEP, STEP), STEP)
+        return pltpu.make_async_remote_copy(
+            src_ref=snd2.at[dest, :, :, pl.ds(pl.multiple_of(q * STEP, STEP), STEP)],
+            dst_ref=out_ref.at[:, :, there],
+            send_sem=s2.at[q, k],
+            recv_sem=r2.at[q, k],
+            device_id={"row": dest},
+            device_id_type=pl.DeviceIdType.MESH,
+        )
+
+    def own_copy(q):
+        there = pl.ds(pl.multiple_of(my_row * cx + q * STEP, STEP), STEP)
+        return pltpu.make_async_copy(
+            snd2.at[my_row, :, :, pl.ds(pl.multiple_of(q * STEP, STEP), STEP)], out_ref.at[:, :, there], own.at[q]
+        )
+
+    greet(n_row, n_col, my_row, my_col)
+
+    def depth_step(q, carry):
+        xs = pl.ds(pl.multiple_of(q * STEP, STEP), STEP)
+        data = halves(f_ref[xs].reshape(STEP * cy, nz))
+        for c in range(n_col):
+            cs = slice(c * width, (c + 1) * width)
+            res = product(data, (tzh[:, cs], tzl[:, cs]))
+            snd1[c, xs] = res.reshape(STEP, cy, width)
+        for k in range(n_col - 1, 0, -1):
+            col_copy(q, k).start()
+        rcv1[my_col, xs] = snd1[my_col, xs]
+        return carry
+
+    lax.fori_loop(0, steps, depth_step, 0)
+
+    def second_step(q, carry):
+        for k in range(1, n_col):
+            col_copy(q, k).wait_recv()
+        parts = []
+        for i in range(STEP):
+            block = jnp.concatenate([rcv1[s, q * STEP + i] for s in range(n_col)], axis=0)
+            parts.append(block.T)
+        data = halves(jnp.concatenate(parts, axis=0))
+        res = product(data, (tyh[...], tyl[...])).reshape(STEP, width, 2 * ny)
+        real = res[:, :half, :ny] + res[:, half:, ny:]
+        imag = res[:, half:, :ny] - res[:, :half, ny:]
+        xs = pl.ds(pl.multiple_of(q * STEP, STEP), STEP)
+        snd2[:, :, 0, xs] = jnp.swapaxes(real, 0, 1).reshape(n_row, planes, STEP, ny)
+        snd2[:, :, 1, xs] = jnp.swapaxes(imag, 0, 1).reshape(n_row, planes, STEP, ny)
+        for k in range(n_row - 1, 0, -1):
+            row_copy(q, k).start()
+        own_copy(q).start()
+        return carry
+
+    lax.fori_loop(0, steps, second_step, 0)
+
+    def finish(q, carry):
+        for k in range(1, n_col):
+            col_copy(q, k).wait_send()
+        for k in range(1, n_row):
+            row_copy(q, k).wait()
+        own_copy(q).wait()
+        return carry
+
+    lax.fori_loop(0, steps, finish, 0)
+
+
+def exchange(field, n_row, n_col, planes):
+    cx, cy, nz = field.shape
+    nx, ny, keep = cx * n_row, cy * n_col, nz // 2
+    width = 2 * keep // n_col
+    order = []
+    for c in range(n_col):
+        order.append([(r * n_col + c) * planes + p for r in range(n_row) for p in range(planes)])
+    columns = []
+    for freqs in order:
+        cos_z, sin_z = waves(nz, freqs)
+        columns += [cos_z, -sin_z]
+    tz = two_parts(np.concatenate(columns, axis=1))
+    ty = two_parts(np.concatenate(waves(ny, np.arange(ny)), axis=1))
+    steps = cx // STEP
+    vmem = pl.BlockSpec(memory_space=pltpu.VMEM)
+    dma = pltpu.SemaphoreType.DMA
+    flops = 6 * (cx * cy * nz * 2 * keep + cx * width * ny * 2 * ny)
+    return pl.pallas_call(
+        functools.partial(exchange_kernel, n_row, n_col, planes),
+        out_shape=jax.ShapeDtypeStruct((planes, 2, nx, ny), F32),
+        in_specs=[vmem] * 5,
+        out_specs=pl.BlockSpec(memory_space=pl.ANY),
+        scratch_shapes=[
+            pltpu.VMEM((n_col, cx, cy, width), F32),
+            pltpu.VMEM((n_col, cx, cy, width), F32),
+            pltpu.VMEM((n_row, planes, 2, cx, ny), F32),
+            dma((steps, n_col)),
+            dma((steps, n_col)),
+            dma((steps, n_row)),
+            dma((steps, n_row)),
+            dma((steps,)),
+        ],
+        compiler_params=pltpu.CompilerParams(
+            collective_id=0, has_side_effects=True, vmem_limit_bytes=48 * MIB
+        ),
+        cost_estimate=pl.CostEstimate(flops=flops, bytes_accessed=8 * cx * cy * nz, transcendentals=0),
+    )(field, *[jnp.asarray(t) for t in tz + ty])
+
+
+def power_kernel(b_ref, shell_ref, txh, txl, fold_ref, power_ref, sums_ref, total):
+    plane = pl.program_id(0)
+    nx, ny = b_ref.shape[2], b_ref.shape[3]
+
+    @pl.when(plane == 0)
+    def _():
+        total[...] = jnp.zeros_like(total)
+
+    data = halves(b_ref[0].reshape(2 * nx, ny))
+    res = product((txh[...], txl[...]), data)
+    power = jnp.square(res[:nx]) + jnp.square(res[nx:])
+    power_ref[0] = power.T
+
+    rows = 64
+
+    def slab(i, carry):
+        rs = pl.ds(pl.multiple_of(i * rows, rows), rows)
+        marks = shell_ref[0, rs]
+        upper, lower = halves(power_ref[0, rs])
+        high = (marks // HALF).astype(F32).astype(BF16)
+        low = (marks % HALF).astype(F32).astype(BF16)
+
+        def wide(values):
+            return jnp.concatenate([values[g * HALF : (g + 1) * HALF] for g in range(rows // HALF)], axis=1)
+
+        upper, lower, high, low = wide(upper), wide(lower), wide(high), wide(low)
+        zero = jnp.zeros_like(upper)
+        one = jnp.ones_like(upper)
+        a = [jnp.where(high == BF16(h), upper, zero) for h in range(HALF)]
+        a += [jnp.where(high == BF16(h), lower, zero) for h in range(HALF)]
+        b = [jnp.where(low == BF16(h), one, zero) for h in range(HALF)]
+        total[...] += lax.dot_general(
+            jnp.concatenate(a, axis=0),
+            jnp.concatenate(b, axis=0),
+            (((1,), (1,)), ((), ())),
+            preferred_element_type=F32,
+        )
+        return carry
+
+    lax.fori_loop(0, ny // rows, slab, 0)
+
+    @pl.when(plane == pl.num_programs(0) - 1)
+    def _():
+        size = HALF * HALF
+        both = total[:size] + total[size:]
+        row = lax.broadcasted_iota(jnp.int32, (size, size), 0) % HALF
+        col = lax.broadcasted_iota(jnp.int32, (size, size), 1) % HALF
+        kept = jnp.where(row == col, both, 0.0).reshape(HALF, HALF, size)
+        sums_ref[...] = jnp.dot(
+            jnp.sum(kept, axis=1), fold_ref[...], precision=HIGH, preferred_element_type=F32
+        )
+
+
+def powers(b, shell):
+    planes, _, nx, ny = b.shape
+    cos_x, sin_x = waves(nx, np.arange(nx))
+    cos_x, sin_x = cos_x.T, sin_x.T
+    tx = two_parts(np.block([[cos_x, sin_x], [-sin_x, cos_x]]))
+    fold = np.zeros((HALF * HALF, 128), np.float32)
+    fold[np.arange(HALF * HALF), np.arange(HALF * HALF) // HALF] = 1.0
+    whole = lambda shape: pl.BlockSpec(shape, lambda i: (0,) * len(shape))
+    return pl.pallas_call(
+        power_kernel,
+        grid=(planes,),
+        out_shape=[
+            jax.ShapeDtypeStruct((planes, ny, nx), F32),
+            jax.ShapeDtypeStruct((HALF, 128), F32),
+        ],
+        in_specs=[
+            pl.BlockSpec((1, 2, nx, ny), lambda i: (i, 0, 0, 0)),
+            pl.BlockSpec((1, ny, nx), lambda i: (i, 0, 0)),
+            whole((2 * nx, 2 * nx)),
+            whole((2 * nx, 2 * nx)),
+            whole((HALF * HALF, 128)),
+        ],
+        out_specs=[pl.BlockSpec((1, ny, nx), lambda i: (i, 0, 0)), whole((HALF, 128))],
+        scratch_shapes=[pltpu.VMEM((2 * HALF * HALF, HALF * HALF), F32)],
+        compiler_params=pltpu.CompilerParams(vmem_limit_bytes=40 * MIB),
+    )(b, shell, *[jnp.asarray(t) for t in tx], jnp.asarray(fold))
+
+
+def sum_kernel(n_row, n_col, x_ref, o_ref, rcv1, mid, rcv2, s1, r1, s2, r2):
+    my_row = lax.axis_index("row")
+    my_col = lax.axis_index("col")
+    greet(n_row, n_col, my_row, my_col)
+
+    def row_copy(k):
+        return pltpu.make_async_remote_copy(
+            src_ref=x_ref,
+            dst_ref=rcv1.at[my_row],
+            send_sem=s1.at[k],
+            recv_sem=r1.at[k],
+            device_id={"row": lax.rem(my_row + k, n_row)},
+            device_id_type=pl.DeviceIdType.MESH,
+        )
+
+    def col_copy(k):
+        return pltpu.make_async_remote_copy(
+            src_ref=mid,
+            dst_ref=rcv2.at[my_col],
+            send_sem=s2.at[k],
+            recv_sem=r2.at[k],
+            device_id={"col": lax.rem(my_col + k, n_col)},
+            device_id_type=pl.DeviceIdType.MESH,
+        )
+
+    for k in range(1, n_row):
+        row_copy(k).start()
+    rcv1[my_row] = x_ref[...]
+    for k in range(1, n_row):
+        row_copy(k).wait_recv()
+    mid[...] = jnp.sum(rcv1[...], axis=0)
+    for k in range(1, n_col):
+        col_copy(k).start()
+    rcv2[my_col] = mid[...]
+    for k in range(1, n_col):
+        col_copy(k).wait_recv()
+    o_ref[...] = jnp.sum(rcv2[...], axis=0)
+    for k in range(1, n_row):
+        row_copy(k).wait_send()
+    for k in range(1, n_col):
+        col_copy(k).wait_send()
+
+
+def sum_all(x, n_row, n_col):
+    vmem = pl.BlockSpec(memory_space=pltpu.VMEM)
+    dma = pltpu.SemaphoreType.DMA
+    return pl.pallas_call(
+        functools.partial(sum_kernel, n_row, n_col),
+        out_shape=jax.ShapeDtypeStruct(x.shape, F32),
+        in_specs=[vmem],
+        out_specs=vmem,
+        scratch_shapes=[
+            pltpu.VMEM((n_row,) + x.shape, F32),
+            pltpu.VMEM(x.shape, F32),
+            pltpu.VMEM((n_col,) + x.shape, F32),
+            dma((n_row,)),
+            dma((n_row,)),
+            dma((n_col,)),
+            dma((n_col,)),
+        ],
+        compiler_params=pltpu.CompilerParams(collective_id=1, has_side_effects=True),
+    )(x)
+
+
+def local(field, shell):
+    fields, cx, cy, nz = field.shape
+    n_row = lax.axis_size("row")
+    n_col = lax.axis_size("col")
+    nx, ny, keep = cx * n_row, cy * n_col, nz // 2
+    planes = keep // (n_row * n_col)
+    fits = fields == 1 and planes % 8 == 0 and (2 * keep // n_col) % 128 == 0
+    fits = fits and cx % STEP == 0 and cy % 8 == 0 and nx % 128 == 0 and ny % 128 == 0
+    if not fits:
+        return general(field, shell)
+    b = exchange(field.reshape(cx, cy, nz), n_row, n_col, planes)
+    power, sums = powers(b, shell)
+    sums = sum_all(sums, n_row, n_col)
+    spectrum = sums[:, :HALF].reshape(1, SHELLS) * (float(SHELLS) / (keep * ny * nx))
+    return (power.reshape(1, planes, ny, nx), spectrum)
+
+
 def solution(mesh):
     in_specs = (P(None, "row", "col", None), P(("row", "col"), None, None))
     out_specs = (P(None, ("row", "col"), None, None), P())

time: 483 us -> 155 us (0.32); the launches traced: 476 us -> 155 us
  matrix products: 234 us -> 0 us
  Pallas kernels: 0 us -> 148 us
  waiting for transfers between devices: 80.7 us -> 0 us
  local copies, waits for them, and re-layouts: 79.8 us -> 5.23 us
  blocking collectives: 36.9 us -> 0 us
  other arithmetic: 23 us -> 0.7 us
  starting transfers between devices: 20.1 us -> 0 us
    dot_general x26 -> x0, matrix products: 234 us -> none  [the longest x16 182 us: add_block(): return summed + jnp.dot(pieces, onehot, preferred_element_type=jnp.float32)]
    pallas_call x0 -> x3, Pallas kernels: none -> 148 us  [the longest x1 116 us: exchange(): pl.pallas_call(functools.partial(exchange_kernel, n_row, n_col, planes),...]
    all_to_all x4 -> x0, waiting for transfers between devices: 80.7 us -> none  [the longest x1 30.8 us: local(): a_re = lax.all_to_all(real, 'col', split_axis=3, concat_axis=3, tiled=True)]
    psum x1 -> x0, blocking collectives: 36.9 us -> none  [local(): sums = lax.psum(sums, ('row', 'col'))]
    all_to_all x4 -> x0, starting transfers between devices: 20.1 us -> none  [the longest x1 6.53 us: local(): a_re = lax.all_to_all(real, 'col', split_axis=3, concat_axis=3, tiled=True)]
    all_to_all x7 -> x0, local copies, waits for them, and re-layouts: 18.8 us -> none  [the longest x2 7.06 us: local(): a_re = lax.all_to_all(real, 'col', split_axis=3, concat_axis=3, tiled=True)]
    unnamed x15 -> x18, local copies, waits for them, and re-layouts: 22.9 us -> 4.59 us
    all_to_all x2 -> x0, other arithmetic: 15.6 us -> none  [the longest x1 7.88 us: local(): a_im = lax.all_to_all(imag, 'col', split_axis=3, concat_axis=3, tiled=True)]
  transfers between devices with their start and end apart: 4 -> 0, of which waited for: 4 -> 0; matrix products, arithmetic and copies ran while one was open for 14% -> 0% of each run, Pallas kernels for 0% -> 0%
where the time goes in v1:
time: 155 us
  Pallas kernels  148 us (95%)
  local copies, waits for them, and re-layouts  5.23 us (3%)
    pallas_call x1, Pallas kernels, exchange(): pl.pallas_call(functools.partial(exchange_kernel, n_row, n_col, planes),...  116 us
    pallas_call x1, Pallas kernels, powers(): pl.pallas_call(power_kernel, grid=(planes,), out_shape=[jax.ShapeDtypeStr...  22.1 us
    pallas_call x1, Pallas kernels, sum_all(): pl.pallas_call(functools.partial(sum_kernel, n_row, n_col), out_shape=jax...  10.4 us
    unnamed x18, local copies, waits for them, and re-layouts  4.59 us

profile of v1, /device:TPU:0, one launch (start us, length us, event | category | flops | bytes accessed | tf_op | source)
XLA Modules:
  0.0 155.0 jit_solution(11830340753867399609)
XLA Ops:
  0.6 0.0 copy-start.5
  0.6 1.0 copy-done.5
  1.7 0.0 copy-start.6
  1.7 1.0 copy-done.6
  2.7 0.0 copy-start.7
  2.7 0.9 copy-done.7
  3.7 0.0 copy-start.8
  3.7 0.9 copy-done.8
  4.6 0.0 copy-start
  4.6 0.0 copy-start.1
  4.6 0.0 copy-start.2
  4.6 0.0 copy-start.3
  4.6 115.9 %shard_map.104.b_ref = f32[8,2,256,256]{3,2,1,0:T(8,128)S(1)} custom-call(f32[32,64,512]{2,1,0:T(8,128)} %bitcast.2, bf16[512,512]{1,0:T(8,128)(2,1)S(1)} %copy-done.6, bf16[512,512]{1,0:T(8,128)(2,1)S(1)} %copy-done.5, bf16[256,512]{1,0:T(8,128)(2,1)S(1)} %copy-done.8, bf16[256,512]{1,0:T(8,128)(2,1)S(1)} %copy-done.7), custom_call_target="tpu_custom_call" | custom-call | flops 6442450944 | bytes 8388608 | tf_op jit(solution)/shard_map/pallas_call | solution.py:252
  120.5 0.0 copy-done
  120.5 0.0 copy-done.1
  120.5 0.0 copy-done.2
  120.5 0.0 copy-done.3
  120.6 22.1 %shard_map.105 = (f32[8,256,256]{2,1,0:T(8,128)}, f32[16,128]{1,0:T(8,128)S(1)}) custom-call(f32[8,2,256,256]{3,2,1,0:T(8,128)S(1)} %shard_map.104.b_ref, s32[8,256,256]{2,1,0:T(8,128)S(1)} %copy-done, bf16[512,512]{1,0:T(8,128)(2,1)S(1)} %copy-done.2, bf16[512,512]{1,0:T(8,128)(2,1)S(1)} %copy-done.1, f32[256,128]{1,0:T(8,128)S(1)} %copy-done.3), custom_call_target="tpu_custom_call" | custom-call | tf_op jit(solution)/shard_map/pallas_call | solution.py:335
  142.6 0.0 copy-start.4
  142.6 0.6 copy-done.4
  143.2 10.4 %shard_map.106 = f32[16,128]{1,0:T(8,128)} custom-call(f32[16,128]{1,0:T(8,128)} %copy-done.4), custom_call_target="tpu_custom_call" | custom-call | tf_op jit(solution)/shard_map/pallas_call | solution.py:401
  153.6 0.7 slice_multiply_fusion
  154.3 0.6 mul.19
Async XLA Ops:
  0.6 1.0 copy-start.5
  1.7 1.0 copy-start.6
  2.7 0.9 copy-start.7
  3.7 0.9 copy-start.8
  4.6 115.9 %copy-start = (s32[8,256,256]{2,1,0:T(8,128)S(1)}, s32[8,256,256]{2,1,0:T(8,128)}, u32[]{:S(2)}) copy-start(s32[8,256,256]{2,1,0:T(8,128)} %shell_ref.1) | copy-start | bytes 6291460
  4.6 115.9 %copy-start.1 = (bf16[512,512]{1,0:T(8,128)(2,1)S(1)}, bf16[512,512]{1,0:T(8,128)(2,1)}, u32[]{:S(2)}) copy-start(bf16[512,512]{1,0:T(8,128)(2,1)} %constant.21.clone.txl) | copy-start | bytes 1572868
  4.6 115.9 %copy-start.2 = (bf16[512,512]{1,0:T(8,128)(2,1)S(1)}, bf16[512,512]{1,0:T(8,128)(2,1)}, u32[]{:S(2)}) copy-start(bf16[512,512]{1,0:T(8,128)(2,1)} %constant.20.clone.txh) | copy-start | bytes 1572868
  4.6 115.9 %copy-start.3 = (f32[256,128]{1,0:T(8,128)S(1)}, f32[256,128]{1,0:T(8,128)}, u32[]{:S(2)}) copy-start(f32[256,128]{1,0:T(8,128)} %constant.22.clone.fold_ref) | copy-start | bytes 393220
  142.6 0.6 copy-start.4

commit v2 on v1

--- a/solution.py
+++ b/solution.py
@@ -103,6 +103,8 @@
 BF16 = jnp.bfloat16
 MIB = 1 << 20
 STEP = 8
+SUB = 4
+WINDOW = 3
 HALF = 16
 
 
@@ -145,7 +147,8 @@
     pl.semaphore_wait(barrier, n_col + n_row - 2)
 
 
-def exchange_kernel(n_row, n_col, planes, f_ref, tzh, tzl, tyh, tyl, out_ref, snd1, rcv1, snd2, s1, r1, s2, r2, own):
+def exchange_kernel(n_row, n_col, planes, f_hbm, tables_hbm, out_ref, scratch):
+    f_ref, tzh, tzl, tyh, tyl, snd1, rcv1, snd2, s1, r1, s2, r2, own, f_sem, t_sem = scratch
     my_row = lax.axis_index("row")
     my_col = lax.axis_index("col")
     cx, cy, nz = f_ref.shape
@@ -153,9 +156,18 @@
     width = rcv1.shape[3]
     half = width // 2
     steps = cx // STEP
+    subs = cx // SUB
+    loads = [
+        pltpu.make_async_copy(src, dst, t_sem.at[i])
+        for i, (src, dst) in enumerate(zip(tables_hbm, (tzh, tzl, tyh, tyl)))
+    ]
+
+    def field_copy(q):
+        xs = pl.ds(q * STEP, STEP)
+        return pltpu.make_async_copy(f_hbm.at[xs], f_ref.at[xs], f_sem.at[q])
 
     def col_copy(q, k):
-        xs = pl.ds(pl.multiple_of(q * STEP, STEP), STEP)
+        xs = pl.ds(q * SUB, SUB)
         dest = lax.rem(my_col + k, n_col)
         return pltpu.make_async_remote_copy(
             src_ref=snd1.at[dest, xs],
@@ -184,25 +196,52 @@
             snd2.at[my_row, :, :, pl.ds(pl.multiple_of(q * STEP, STEP), STEP)], out_ref.at[:, :, there], own.at[q]
         )
 
+    def col_start(j):
+        for k in range(n_col - 1, 0, -1):
+            col_copy(j, k).start()
+
+    loads[0].start()
+    loads[1].start()
+    for q in range(steps):
+        field_copy(q).start()
+    loads[2].start()
+    loads[3].start()
     greet(n_row, n_col, my_row, my_col)
+    loads[0].wait()
+    loads[1].wait()
 
     def depth_step(q, carry):
+        field_copy(q).wait()
         xs = pl.ds(pl.multiple_of(q * STEP, STEP), STEP)
         data = halves(f_ref[xs].reshape(STEP * cy, nz))
         for c in range(n_col):
             cs = slice(c * width, (c + 1) * width)
             res = product(data, (tzh[:, cs], tzl[:, cs]))
             snd1[c, xs] = res.reshape(STEP, cy, width)
-        for k in range(n_col - 1, 0, -1):
-            col_copy(q, k).start()
+        for i in range(STEP // SUB):
+            j = q * (STEP // SUB) + i
+
+            @pl.when(j < WINDOW)
+            def _():
+                col_start(j)
+
         rcv1[my_col, xs] = snd1[my_col, xs]
         return carry
 
     lax.fori_loop(0, steps, depth_step, 0)
+    loads[2].wait()
+    loads[3].wait()
 
     def second_step(q, carry):
-        for k in range(1, n_col):
-            col_copy(q, k).wait_recv()
+        for i in range(STEP // SUB):
+            j = q * (STEP // SUB) + i
+            for k in range(1, n_col):
+                col_copy(j, k).wait_recv()
+
+            @pl.when(j + WINDOW < subs)
+            def _():
+                col_start(j + WINDOW)
+
         parts = []
         for i in range(STEP):
             block = jnp.concatenate([rcv1[s, q * STEP + i] for s in range(n_col)], axis=0)
@@ -222,8 +261,9 @@
     lax.fori_loop(0, steps, second_step, 0)
 
     def finish(q, carry):
-        for k in range(1, n_col):
-            col_copy(q, k).wait_send()
+        for i in range(STEP // SUB):
+            for k in range(1, n_col):
+                col_copy(q * (STEP // SUB) + i, k).wait_send()
         for k in range(1, n_row):
             row_copy(q, k).wait()
         own_copy(q).wait()
@@ -246,32 +286,40 @@
     tz = two_parts(np.concatenate(columns, axis=1))
     ty = two_parts(np.concatenate(waves(ny, np.arange(ny)), axis=1))
     steps = cx // STEP
-    vmem = pl.BlockSpec(memory_space=pltpu.VMEM)
     dma = pltpu.SemaphoreType.DMA
     flops = 6 * (cx * cy * nz * 2 * keep + cx * width * ny * 2 * ny)
+    subs = cx // SUB
+
+    def body(f, a, b, c, d, out, *scratch):
+        exchange_kernel(n_row, n_col, planes, f, (a, b, c, d), out, scratch)
+
     return pl.pallas_call(
-        functools.partial(exchange_kernel, n_row, n_col, planes),
+        body,
         out_shape=jax.ShapeDtypeStruct((planes, 2, nx, ny), F32),
-        in_specs=[vmem] * 5,
+        in_specs=[pl.BlockSpec(memory_space=pl.ANY)] * 5,
         out_specs=pl.BlockSpec(memory_space=pl.ANY),
         scratch_shapes=[
+            pltpu.VMEM((cx, cy, nz), F32),
+            *[pltpu.VMEM(t.shape, BF16) for t in tz + ty],
             pltpu.VMEM((n_col, cx, cy, width), F32),
             pltpu.VMEM((n_col, cx, cy, width), F32),
             pltpu.VMEM((n_row, planes, 2, cx, ny), F32),
-            dma((steps, n_col)),
-            dma((steps, n_col)),
+            dma((subs, n_col)),
+            dma((subs, n_col)),
             dma((steps, n_row)),
             dma((steps, n_row)),
             dma((steps,)),
+            dma((steps,)),
+            dma((4,)),
         ],
         compiler_params=pltpu.CompilerParams(
-            collective_id=0, has_side_effects=True, vmem_limit_bytes=48 * MIB
+            collective_id=0, has_side_effects=True, vmem_limit_bytes=60 * MIB
         ),
         cost_estimate=pl.CostEstimate(flops=flops, bytes_accessed=8 * cx * cy * nz, transcendentals=0),
     )(field, *[jnp.asarray(t) for t in tz + ty])
 
 
-def power_kernel(b_ref, shell_ref, txh, txl, fold_ref, power_ref, sums_ref, total):
+def power_kernel(scale, b_ref, shell_ref, txh, txl, fold_ref, power_ref, sums_ref, total):
     plane = pl.program_id(0)
     nx, ny = b_ref.shape[2], b_ref.shape[3]
 
@@ -284,7 +332,7 @@
     power = jnp.square(res[:nx]) + jnp.square(res[nx:])
     power_ref[0] = power.T
 
-    rows = 64
+    rows = min(ny, 128)
 
     def slab(i, carry):
         rs = pl.ds(pl.multiple_of(i * rows, rows), rows)
@@ -319,36 +367,40 @@
         row = lax.broadcasted_iota(jnp.int32, (size, size), 0) % HALF
         col = lax.broadcasted_iota(jnp.int32, (size, size), 1) % HALF
         kept = jnp.where(row == col, both, 0.0).reshape(HALF, HALF, size)
-        sums_ref[...] = jnp.dot(
+        folded = jnp.dot(
             jnp.sum(kept, axis=1), fold_ref[...], precision=HIGH, preferred_element_type=F32
         )
-
-
-def powers(b, shell):
+        at_high = lax.broadcasted_iota(jnp.int32, (HALF, size), 0)
+        of_shell = lax.broadcasted_iota(jnp.int32, (HALF, size), 1) // HALF
+        found = jnp.where(at_high == of_shell, folded, 0.0)
+        sums_ref[...] = jnp.sum(found, axis=0, keepdims=True) * scale
+
+
+def powers(b, shell, scale):
     planes, _, nx, ny = b.shape
     cos_x, sin_x = waves(nx, np.arange(nx))
     cos_x, sin_x = cos_x.T, sin_x.T
     tx = two_parts(np.block([[cos_x, sin_x], [-sin_x, cos_x]]))
-    fold = np.zeros((HALF * HALF, 128), np.float32)
-    fold[np.arange(HALF * HALF), np.arange(HALF * HALF) // HALF] = 1.0
+    ids = np.arange(HALF * HALF)
+    fold = (ids[:, None] // HALF == ids[None, :] % HALF).astype(np.float32)
     whole = lambda shape: pl.BlockSpec(shape, lambda i: (0,) * len(shape))
     return pl.pallas_call(
-        power_kernel,
+        functools.partial(power_kernel, scale),
         grid=(planes,),
         out_shape=[
             jax.ShapeDtypeStruct((planes, ny, nx), F32),
-            jax.ShapeDtypeStruct((HALF, 128), F32),
+            jax.ShapeDtypeStruct((1, HALF * HALF), F32),
         ],
         in_specs=[
             pl.BlockSpec((1, 2, nx, ny), lambda i: (i, 0, 0, 0)),
             pl.BlockSpec((1, ny, nx), lambda i: (i, 0, 0)),
             whole((2 * nx, 2 * nx)),
             whole((2 * nx, 2 * nx)),
-            whole((HALF * HALF, 128)),
+            whole((HALF * HALF, HALF * HALF)),
         ],
-        out_specs=[pl.BlockSpec((1, ny, nx), lambda i: (i, 0, 0)), whole((HALF, 128))],
+        out_specs=[pl.BlockSpec((1, ny, nx), lambda i: (i, 0, 0)), whole((1, HALF * HALF))],
         scratch_shapes=[pltpu.VMEM((2 * HALF * HALF, HALF * HALF), F32)],
-        compiler_params=pltpu.CompilerParams(vmem_limit_bytes=40 * MIB),
+        compiler_params=pltpu.CompilerParams(vmem_limit_bytes=60 * MIB),
     )(b, shell, *[jnp.asarray(t) for t in tx], jnp.asarray(fold))
 
 
@@ -424,12 +476,12 @@
     planes = keep // (n_row * n_col)
     fits = fields == 1 and planes % 8 == 0 and (2 * keep // n_col) % 128 == 0
     fits = fits and cx % STEP == 0 and cy % 8 == 0 and nx % 128 == 0 and ny % 128 == 0
+    fits = fits and SHELLS == HALF * HALF
     if not fits:
         return general(field, shell)
     b = exchange(field.reshape(cx, cy, nz), n_row, n_col, planes)
-    power, sums = powers(b, shell)
-    sums = sum_all(sums, n_row, n_col)
-    spectrum = sums[:, :HALF].reshape(1, SHELLS) * (float(SHELLS) / (keep * ny * nx))
+    power, sums = powers(b, shell, float(SHELLS) / (keep * ny * nx))
+    spectrum = sum_all(sums, n_row, n_col)
     return (power.reshape(1, planes, ny, nx), spectrum)
 
 

time: 155 us -> 147 us (0.948)
  local copies, waits for them, and re-layouts: 5.23 us -> 1.22 us
  Pallas kernels: 148 us -> 145 us
    unnamed x18 -> x1, local copies, waits for them, and re-layouts: 4.59 us -> 1.22 us
    pallas_call x2, Pallas kernels: 138 us -> 135 us  [the longest x1 114 us: exchange(): pl.pallas_call(body, out_shape=jax.ShapeDtypeStruct((planes, 2, nx, ny),...]
where the time goes in v2:
time: 147 us; the launch traced here: 146 us
  Pallas kernels  145 us (99%)
    pallas_call x1, Pallas kernels, exchange(): pl.pallas_call(body, out_shape=jax.ShapeDtypeStruct((planes, 2, nx, ny),...  114 us
    pallas_call x1, Pallas kernels, powers(): pl.pallas_call(functools.partial(power_kernel, scale), grid=(planes,), ou...  20.3 us
    pallas_call x1, Pallas kernels, sum_all(): pl.pallas_call(functools.partial(sum_kernel, n_row, n_col), out_shape=jax...  9.9 us

profile of v2, /device:TPU:0, one launch (start us, length us, event | category | flops | bytes accessed | tf_op | source)
XLA Modules:
  0.0 146.5 jit_solution(8976385055652721511)
XLA Ops:
  0.6 114.4 %shard_map.104.b_ref = f32[8,2,256,256]{3,2,1,0:T(8,128)} custom-call(f32[32,64,512]{2,1,0:T(8,128)} %bitcast.2, bf16[512,512]{1,0:T(8,128)(2,1)} %constant.14.clone.a, bf16[512,512]{1,0:T(8,128)(2,1)} %constant.15.clone.b, bf16[256,512]{1,0:T(8,128)(2,1)} %constant.16.clone.c, bf16[256,512]{1,0:T(8,128)(2,1)} %constant.17.clone.d), custom_call_target="tpu_custom_call" | custom-call | flops 6442450944 | bytes 8388608 | tf_op jit(solution)/shard_map/pallas_call | solution.py:296
  115.1 20.3 %shard_map.105 = (f32[8,256,256]{2,1,0:T(8,128)}, f32[1,256]{1,0:T(1,128)}) custom-call(f32[8,2,256,256]{3,2,1,0:T(8,128)} %shard_map.104.b_ref, s32[8,256,256]{2,1,0:T(8,128)} %shell_ref.1, bf16[512,512]{1,0:T(8,128)(2,1)} %constant.18.clone.txh, bf16[512,512]{1,0:T(8,128)(2,1)} %constant.19.clone.txl, f32[256,256]{1,0:T(8,128)} %constant.20.clone.fold_ref), custom_call_target="tpu_custom_call" | custom-call | tf_op jit(solution)/shard_map/pallas_call | solution.py:387
  135.4 9.9 %shard_map.106 = f32[1,256]{1,0:T(1,128)} custom-call(f32[1,256]{1,0:T(1,128)} %get-tuple-element.5.x_ref), custom_call_target="tpu_custom_call" | custom-call | tf_op jit(solution)/shard_map/pallas_call | solution.py:453
  145.3 1.2 copy.12

commit v3 on v2

--- a/solution.py
+++ b/solution.py
@@ -104,7 +104,7 @@
 MIB = 1 << 20
 STEP = 8
 SUB = 4
-WINDOW = 3
+WINDOW = 2
 HALF = 16
 
 
@@ -332,7 +332,7 @@
     power = jnp.square(res[:nx]) + jnp.square(res[nx:])
     power_ref[0] = power.T
 
-    rows = min(ny, 128)
+    rows = min(ny, 256)
 
     def slab(i, carry):
         rs = pl.ds(pl.multiple_of(i * rows, rows), rows)
@@ -476,7 +476,7 @@
     planes = keep // (n_row * n_col)
     fits = fields == 1 and planes % 8 == 0 and (2 * keep // n_col) % 128 == 0
     fits = fits and cx % STEP == 0 and cy % 8 == 0 and nx % 128 == 0 and ny % 128 == 0
-    fits = fits and SHELLS == HALF * HALF
+    fits = fits and SHELLS == HALF * HALF and ny % min(ny, 256) == 0
     if not fits:
         return general(field, shell)
     b = exchange(field.reshape(cx, cy, nz), n_row, n_col, planes)

time: 147 us -> 152 us (1.034)
  Pallas kernels: 145 us -> 150 us
    pallas_call x1, Pallas kernels: 20.3 us -> 24 us  [powers(): pl.pallas_call(functools.partial(power_kernel, scale), grid=(planes,), ou...]
where the time goes in v3:
time: 152 us
  Pallas kernels  150 us (99%)
    pallas_call x1, Pallas kernels, exchange(): pl.pallas_call(body, out_shape=jax.ShapeDtypeStruct((planes, 2, nx, ny),...  114 us
    pallas_call x1, Pallas kernels, powers(): pl.pallas_call(functools.partial(power_kernel, scale), grid=(planes,), ou...  24 us
    pallas_call x1, Pallas kernels, sum_all(): pl.pallas_call(functools.partial(sum_kernel, n_row, n_col), out_shape=jax...  11.2 us

profile of v3, /device:TPU:0, one launch (start us, length us, event | category | flops | bytes accessed | tf_op | source)
XLA Modules:
  0.0 151.6 jit_solution(66195517750416525)
XLA Ops:
  0.6 114.5 %shard_map.104.b_ref = f32[8,2,256,256]{3,2,1,0:T(8,128)} custom-call(f32[32,64,512]{2,1,0:T(8,128)} %bitcast.2, bf16[512,512]{1,0:T(8,128)(2,1)} %constant.14.clone.a, bf16[512,512]{1,0:T(8,128)(2,1)} %constant.15.clone.b, bf16[256,512]{1,0:T(8,128)(2,1)} %constant.16.clone.c, bf16[256,512]{1,0:T(8,128)(2,1)} %constant.17.clone.d), custom_call_target="tpu_custom_call" | custom-call | flops 6442450944 | bytes 8388608 | tf_op jit(solution)/shard_map/pallas_call | solution.py:296
  115.1 24.0 %shard_map.105 = (f32[8,256,256]{2,1,0:T(8,128)}, f32[1,256]{1,0:T(1,128)}) custom-call(f32[8,2,256,256]{3,2,1,0:T(8,128)} %shard_map.104.b_ref, s32[8,256,256]{2,1,0:T(8,128)} %shell_ref.1, bf16[512,512]{1,0:T(8,128)(2,1)} %constant.18.clone.txh, bf16[512,512]{1,0:T(8,128)(2,1)} %constant.19.clone.txl, f32[256,256]{1,0:T(8,128)} %constant.20.clone.fold_ref), custom_call_target="tpu_custom_call" | custom-call | tf_op jit(solution)/shard_map/pallas_call | solution.py:387
  139.1 11.2 %shard_map.106 = f32[1,256]{1,0:T(1,128)} custom-call(f32[1,256]{1,0:T(1,128)} %get-tuple-element.5.x_ref), custom_call_target="tpu_custom_call" | custom-call | tf_op jit(solution)/shard_map/pallas_call | solution.py:453
  150.4 1.2 copy.12
